TPU v7x, 128 devices: a whole 4x4x4 slice. The times are simulated.
128 devices in a mesh: shards: 8 (over x, z_lo), context: 16 (over y, z_hi, core).
Axes of the slice: x: 4, y: 4, z: 4 (z_hi: 2, z_lo: 2; z = z_hi * 2 + z_lo), core: 2. Of those that a mesh axis runs over, the one named last changes fastest.
Arguments:
- hidden_in: bfloat16 [8, 2048, 1024], P('shards', 'context'), may hold values from -6 to 6
- ln_gain: float32 [2, 1024], replicated, may hold values from 0.5 to 1.5
- ln_bias: float32 [2, 1024], replicated, may hold values from -1.75 to 1.75
- qkv_weight: bfloat16 [2, 1024, 16, 192], P(None, 'shards', 'context'), may hold values from -0.1875 to 0.1875
- qkv_bias: float32 [2, 16, 192], replicated, may hold values from -1.75 to 1.75
- out_weight: bfloat16 [2, 16, 64, 1024], P(None, 'context', None, 'shards'), may hold values from -1.5 to 1.5
- out_bias: float32 [2, 1024], replicated, may hold values from -1.75 to 1.75
- fc1_weight: bfloat16 [2, 1024, 4096], P(None, 'shards', 'context'), may hold values from -0.1875 to 0.1875
- fc1_bias: float32 [2, 4096], replicated, may hold values from -3 to 3
- fc2_weight: bfloat16 [2, 4096, 1024], P(None, 'context', 'shards'), may hold values from -0.09375 to 0.09375
- fc2_bias: float32 [2, 1024], replicated, may hold values from -1.75 to 1.75
- cotangent: bfloat16 [8, 2048, 1024], P('shards', 'context'), may hold values from -6 to 6
Outputs:
- hidden_out: bfloat16 [8, 2048, 1024], P('shards', 'context')
- grad_in: float32 [8, 2048, 1024], P('shards', 'context')
- grad_ln_gain: float32 [2, 1024], replicated
- grad_ln_bias: float32 [2, 1024], replicated
- grad_qkv_weight: float32 [2, 1024, 16, 192], P(None, 'shards', 'context')
- grad_qkv_bias: float32 [2, 16, 192], replicated
- grad_out_weight: float32 [2, 16, 64, 1024], P(None, 'context', None, 'shards')
- grad_out_bias: float32 [2, 1024], replicated
- grad_fc1_weight: float32 [2, 1024, 4096], P(None, 'shards', 'context')
- grad_fc1_bias: float32 [2, 4096], replicated
- grad_fc2_weight: float32 [2, 4096, 1024], P(None, 'context', 'shards')
- grad_fc2_bias: float32 [2, 1024], replicated
All inputs are finite; a program needn't handle non-finite values.
Results may differ from a plain program's by a relative error of at most 0.028.
Values may be sent and summed in bfloat16 or wider, within the bound.
A program may use at most 192 MiB of HBM per device.

v0:
```python
import jax
import jax.numpy as jnp
from jax import lax
from jax.sharding import PartitionSpec as P

HD = 64
ROT = 16


EPSILON = 1e-05
MASKED = -1e30


def norm_parts(rows_in, gain_vec, shift_vec):
    row_mean = jnp.mean(rows_in, axis=-1, keepdims=True)
    centered = rows_in - row_mean
    variance = jnp.mean(centered * centered, axis=-1, keepdims=True)
    inverse = lax.rsqrt(variance + EPSILON)
    normal = centered * inverse
    return (normal * gain_vec + shift_vec, normal, inverse)


def norm_back(grad_normed, normal, inverse, gain_vec):
    scaled = grad_normed * gain_vec
    first_mean = jnp.mean(scaled, axis=-1, keepdims=True)
    cross_mean = jnp.mean(scaled * normal, axis=-1, keepdims=True)
    return inverse * (scaled - first_mean - normal * cross_mean)


def rotary_tables(length):
    frequency = 1.0 / 10000.0 ** (jnp.arange(0, ROT, 2).astype(jnp.float32) / ROT)
    angles = jnp.arange(length).astype(jnp.float32)[:, None] * frequency[None, :]
    return (jnp.cos(angles)[:, None, :], jnp.sin(angles)[:, None, :])


def rotate(section, cosine, sine_table):
    half_rot = ROT // 2
    front_half = section[..., :half_rot]
    back_half = section[..., half_rot:ROT]
    remainder = section[..., ROT:]
    return jnp.concatenate(
        [
            front_half * cosine - back_half * sine_table,
            back_half * cosine + front_half * sine_table,
            remainder,
        ],
        axis=-1,
    )


def unrotate(section, cosine, sine_table):
    half_rot = ROT // 2
    front_half = section[..., :half_rot]
    back_half = section[..., half_rot:ROT]
    remainder = section[..., ROT:]
    return jnp.concatenate(
        [
            front_half * cosine + back_half * sine_table,
            back_half * cosine - front_half * sine_table,
            remainder,
        ],
        axis=-1,
    )


def causal_scores(queries, key_rows, begin_row, block_rows):
    end_row = begin_row + block_rows
    scores = jnp.einsum(
        "qhd,khd->hqk",
        queries[begin_row:end_row],
        key_rows[:end_row],
        preferred_element_type=jnp.float32,
    ) * HD ** (-0.5)
    allowed = jnp.arange(end_row)[None, :] <= (begin_row + jnp.arange(block_rows))[:, None]
    return jnp.where(allowed[None], scores, MASKED)


def attend(queries, key_rows, values):
    length = queries.shape[0]
    block_rows = min(512, length)
    outputs = []
    log_sums = []
    for block_index in range(length // block_rows):
        begin_row = block_index * block_rows
        end_row = begin_row + block_rows
        scores = causal_scores(queries, key_rows, begin_row, block_rows)
        row_peak = jnp.max(scores, axis=-1, keepdims=True)
        exp_terms = jnp.exp(scores - row_peak)
        row_total = jnp.sum(exp_terms, axis=-1, keepdims=True)
        weights = (exp_terms / row_total).astype(jnp.bfloat16)
        outputs.append(
            jnp.einsum(
                "hqk,khd->qhd", weights, values[:end_row], preferred_element_type=jnp.float32
            )
        )
        log_sums.append(row_peak + jnp.log(row_total))
    return (jnp.concatenate(outputs, axis=0), log_sums)


def attend_back(queries, key_rows, values, grad_mixed, log_sums):
    length = queries.shape[0]
    block_rows = min(512, length)
    scaling = HD ** (-0.5)
    grad_queries = []
    grad_keys = jnp.zeros(key_rows.shape, jnp.float32)
    grad_values = jnp.zeros(values.shape, jnp.float32)
    for block_index in range(length // block_rows):
        begin_row = block_index * block_rows
        end_row = begin_row + block_rows
        scores = causal_scores(queries, key_rows, begin_row, block_rows)
        probabilities = jnp.exp(scores - log_sums[block_index])
        grad_block = grad_mixed[begin_row:end_row]
        grad_probs = jnp.einsum(
            "qhd,khd->hqk", grad_block, values[:end_row], preferred_element_type=jnp.float32
        )
        row_delta = jnp.sum(probabilities * grad_probs, axis=-1, keepdims=True)
        grad_scores = (probabilities * (grad_probs - row_delta)).astype(jnp.bfloat16)
        grad_queries.append(
            jnp.einsum(
                "hqk,khd->qhd", grad_scores, key_rows[:end_row], preferred_element_type=jnp.float32
            )
            * scaling
        )
        grad_keys = grad_keys.at[:end_row].add(
            jnp.einsum(
                "hqk,qhd->khd",
                grad_scores,
                queries[begin_row:end_row],
                preferred_element_type=jnp.float32,
            )
            * scaling
        )
        grad_values = grad_values.at[:end_row].add(
            jnp.einsum(
                "hqk,qhd->khd",
                probabilities.astype(jnp.bfloat16),
                grad_block,
                preferred_element_type=jnp.float32,
            )
        )
    return (jnp.concatenate(grad_queries, axis=0), grad_keys, grad_values)


def gelu_exact(value):
    return jax.nn.gelu(value, approximate=False)


def forward_local(normed_low, full_weights, bias_qkv, bias_up, cosine, sine_table):
    w_qkv = full_weights[0]
    w_up = full_weights[2]
    projected = (
        jnp.einsum("td,dhe->the", normed_low, w_qkv, preferred_element_type=jnp.float32) + bias_qkv
    )
    queries = rotate(projected[..., :HD], cosine, sine_table).astype(jnp.bfloat16)
    key_rows = rotate(projected[..., HD : 2 * HD], cosine, sine_table).astype(jnp.bfloat16)
    values = projected[..., 2 * HD :].astype(jnp.bfloat16)
    mixed, log_sums = attend(queries, key_rows, values)
    hidden = jnp.dot(normed_low, w_up, preferred_element_type=jnp.float32) + bias_up
    active_low = gelu_exact(hidden).astype(jnp.bfloat16)
    return (queries, key_rows, values, log_sums, mixed.astype(jnp.bfloat16), hidden, active_low)


def branch_rows(mixed_low, active_low, w_out, w_down):
    return jnp.einsum(
        "thd,hde->te", mixed_low, w_out, preferred_element_type=jnp.float32
    ) + jnp.dot(active_low, w_down, preferred_element_type=jnp.float32)


def normed_grad_rows(grad_proj, grad_hidden, w_qkv, w_up):
    return jnp.einsum(
        "the,dhe->td", grad_proj, w_qkv, preferred_element_type=jnp.float32
    ) + jnp.einsum("tf,df->td", grad_hidden, w_up, preferred_element_type=jnp.float32)


def gather_cotangent(rows_low):
    return lax.all_gather(rows_low, "context", axis=0, tiled=True)


def on_device(
    hidden_in,
    ln_gain,
    ln_bias,
    qkv_weight,
    qkv_bias,
    out_weight,
    out_bias,
    fc1_weight,
    fc1_bias,
    fc2_weight,
    fc2_bias,
    cotangent,
):
    ctx_index = lax.axis_index("context")
    tokens = hidden_in.shape[1]
    length = tokens * lax.axis_size("context")
    layers = qkv_weight.shape[0]
    heads_here = qkv_weight.shape[2]
    units_here = fc1_weight.shape[2]
    first_row = ctx_index * tokens
    cosine, sine_table = rotary_tables(length)
    stream = lax.all_gather(hidden_in[0], "context", axis=0, tiled=True).astype(jnp.float32)
    saved = []
    for layer_index in range(layers):
        full_weights = (
            lax.all_gather(qkv_weight[layer_index], "shards", axis=0, tiled=True),
            lax.all_gather(out_weight[layer_index], "shards", axis=2, tiled=True),
            lax.all_gather(fc1_weight[layer_index], "shards", axis=0, tiled=True),
            lax.all_gather(fc2_weight[layer_index], "shards", axis=1, tiled=True),
        )
        normed, normal, inverse = norm_parts(stream, ln_gain[layer_index], ln_bias[layer_index])
        normed_low = normed.astype(jnp.bfloat16)
        bias_qkv = lax.dynamic_slice_in_dim(
            qkv_bias[layer_index], ctx_index * heads_here, heads_here, 0
        )
        bias_up = lax.dynamic_slice_in_dim(
            fc1_bias[layer_index], ctx_index * units_here, units_here, 0
        )
        kept_state = forward_local(normed_low, full_weights, bias_qkv, bias_up, cosine, sine_table)
        mixed_low = kept_state[4]
        active_low = kept_state[6]
        branch = lax.psum(
            branch_rows(mixed_low, active_low, full_weights[1], full_weights[3]).astype(
                jnp.bfloat16
            ),
            "context",
        ).astype(jnp.float32)
        saved.append((normal, inverse, normed_low, full_weights, kept_state))
        stream = stream + branch + out_bias[layer_index] + fc2_bias[layer_index]
    result_rows = lax.dynamic_slice_in_dim(stream, first_row, tokens, 0)
    grad_stream = gather_cotangent(cotangent[0]).astype(jnp.float32)
    hidden_out = result_rows.astype(jnp.bfloat16)[None]
    gain_grads = [None] * layers
    shift_grads = [None] * layers
    qkv_bias_grads = [None] * layers
    bias_grads = [None] * layers
    up_bias_grads = [None] * layers
    qkv_grads = [None] * layers
    out_grads = [None] * layers
    up_grads = [None] * layers
    down_grads = [None] * layers
    for layer_index in reversed(range(layers)):
        normal, inverse, normed_low, full_weights, kept_state = saved[layer_index]
        w_qkv, w_out, w_up, w_down = full_weights
        queries, key_rows, values, log_sums, mixed_low, hidden, active_low = kept_state
        grad_low = grad_stream.astype(jnp.bfloat16)
        own_low = lax.dynamic_slice_in_dim(grad_low, first_row, tokens, 0)
        bias_grads[layer_index] = jnp.sum(own_low.astype(jnp.float32), axis=0)
        grad_mixed = jnp.einsum(
            "te,hde->thd", grad_low, w_out, preferred_element_type=jnp.float32
        ).astype(jnp.bfloat16)
        grad_w_out = jnp.einsum(
            "thd,te->hde", mixed_low, grad_low, preferred_element_type=jnp.float32
        )
        grad_active = jnp.einsum("te,fe->tf", grad_low, w_down, preferred_element_type=jnp.float32)
        grad_w_down = jnp.einsum(
            "tf,te->fe", active_low, grad_low, preferred_element_type=jnp.float32
        )
        grad_hidden = jax.vjp(gelu_exact, hidden)[1](grad_active)[0].astype(jnp.bfloat16)
        grad_queries, grad_keys, grad_values = attend_back(
            queries, key_rows, values, grad_mixed, log_sums
        )
        grad_proj = jnp.concatenate(
            [
                unrotate(grad_queries, cosine, sine_table),
                unrotate(grad_keys, cosine, sine_table),
                grad_values,
            ],
            axis=-1,
        ).astype(jnp.bfloat16)
        proj_sums = jnp.sum(grad_proj.astype(jnp.float32), axis=0)
        qkv_bias_grads[layer_index] = lax.dynamic_update_slice_in_dim(
            jnp.zeros(qkv_bias.shape[1:], jnp.float32), proj_sums, ctx_index * heads_here, 0
        )
        up_here = jnp.sum(grad_hidden.astype(jnp.float32), axis=0)
        up_bias_grads[layer_index] = lax.dynamic_update_slice_in_dim(
            jnp.zeros(fc1_bias.shape[1:], jnp.float32), up_here, ctx_index * units_here, 0
        )
        grad_w_qkv = jnp.einsum(
            "td,the->dhe", normed_low, grad_proj, preferred_element_type=jnp.float32
        )
        grad_w_up = jnp.einsum(
            "td,tf->df", normed_low, grad_hidden, preferred_element_type=jnp.float32
        )
        owned = (
            lax.psum_scatter(
                grad_w_qkv.astype(jnp.bfloat16), "shards", scatter_dimension=0, tiled=True
            ).astype(jnp.float32),
            lax.psum_scatter(
                grad_w_out.astype(jnp.bfloat16), "shards", scatter_dimension=2, tiled=True
            ).astype(jnp.float32),
            lax.psum_scatter(
                grad_w_up.astype(jnp.bfloat16), "shards", scatter_dimension=0, tiled=True
            ).astype(jnp.float32),
            lax.psum_scatter(
                grad_w_down.astype(jnp.bfloat16), "shards", scatter_dimension=1, tiled=True
            ).astype(jnp.float32),
        )
        qkv_grads[layer_index] = owned[0]
        out_grads[layer_index] = owned[1]
        up_grads[layer_index] = owned[2]
        down_grads[layer_index] = owned[3]
        grad_normed = lax.psum(
            normed_grad_rows(grad_proj, grad_hidden, w_qkv, w_up).astype(jnp.bfloat16), "context"
        ).astype(jnp.float32)
        own_grad = lax.dynamic_slice_in_dim(grad_normed, first_row, tokens, 0)
        own_normal = lax.dynamic_slice_in_dim(normal, first_row, tokens, 0)
        gain_grads[layer_index] = jnp.sum(own_grad * own_normal, axis=0)
        shift_grads[layer_index] = jnp.sum(own_grad, axis=0)
        grad_stream = grad_stream + norm_back(grad_normed, normal, inverse, ln_gain[layer_index])
    grad_rows = lax.dynamic_slice_in_dim(grad_stream, first_row, tokens, 0)
    vector_sums = lax.psum(
        (
            jnp.stack(gain_grads),
            jnp.stack(shift_grads),
            jnp.stack(qkv_bias_grads),
            jnp.stack(bias_grads),
            jnp.stack(up_bias_grads),
        ),
        ("shards", "context"),
    )
    return (
        hidden_out,
        grad_rows[None],
        vector_sums[0],
        vector_sums[1],
        jnp.stack(qkv_grads),
        vector_sums[2],
        jnp.stack(out_grads),
        vector_sums[3],
        jnp.stack(up_grads),
        vector_sums[4],
        jnp.stack(down_grads),
        vector_sums[3],
    )


def solution(mesh):
    placed = (
        P("shards", "context", None),
        P(),
        P(),
        P(None, "shards", "context", None),
        P(),
        P(None, "context", None, "shards"),
        P(),
        P(None, "shards", "context"),
        P(),
        P(None, "context", "shards"),
        P(),
        P("shards", "context", None),
    )
    return jax.shard_map(
        on_device,
        mesh=mesh,
        in_specs=placed,
        out_specs=(
            P("shards", "context", None),
            P("shards", "context", None),
            P(),
            P(),
            P(None, "shards", "context", None),
            P(),
            P(None, "context", None, "shards"),
            P(),
            P(None, "shards", "context"),
            P(),
            P(None, "context", "shards"),
            P(),
        ),
        check_vma=False,
    )
```

profile of v0, /device:TPU:1, one launch (start us, length us, event | category | flops | bytes accessed | tf_op | source)
XLA Modules:
  0.0 1208.6 jit_solution(12988790611949388414)
XLA Ops:
  8.8 1.4 fusion.284
  10.2 1.4 fusion.285
  14.2 1.5 fusion.281
  15.7 1.4 fusion.280
  17.1 21.2 %all-gather.2 = bf16[1,1,64,1024]{3,2,1,0:T(8,128)(2,1)S(1)} all-gather(bf16[1,1,64,128]{3,2,1,0:T(8,128)(2,1)S(1)} %get-tuple-element.303), channel_id=4, replica_groups=mesh['shards'=8,'context'=16] {'shards'}, dimensions={3}, use_global_device_ids=true | all-gather | bytes 147456 | tf_op jit(solution)/shard_map/all_gather | solution.py:206
  38.3 1.6 fusion.279
  39.9 1.5 fusion.278
  41.4 21.9 %all-gather.1 = bf16[1,1024,1,192]{1,3,2,0:T(8,128)(2,1)S(1)} all-gather(bf16[1,128,1,192]{1,3,2,0:T(8,128)(2,1)S(1)} %get-tuple-element.297), channel_id=3, replica_groups=mesh['shards'=8,'context'=16] {'shards'}, dimensions={1}, use_global_device_ids=true | all-gather | bytes 442368 | tf_op jit(solution)/shard_map/all_gather | solution.py:205
  63.2 22.8 %all-gather.4 = bf16[1,256,1024]{2,1,0:T(8,128)(2,1)} all-gather(bf16[1,256,128]{2,1,0:T(8,128)(2,1)S(1)} %get-tuple-element.293), channel_id=6, replica_groups=mesh['shards'=8,'context'=16] {'shards'}, dimensions={2}, use_global_device_ids=true | all-gather | bytes 589824 | tf_op jit(solution)/shard_map/all_gather | solution.py:208
  86.1 25.1 %all-gather.3 = bf16[1,1024,256]{2,1,0:T(8,128)(2,1)} all-gather(bf16[1,128,256]{2,1,0:T(8,128)(2,1)S(1)} %get-tuple-element.295), channel_id=5, replica_groups=mesh['shards'=8,'context'=16] {'shards'}, dimensions={1}, use_global_device_ids=true | all-gather | bytes 589824 | tf_op jit(solution)/shard_map/all_gather | solution.py:207
  111.7 3.0 convert_reduce_fusion
  115.2 1.4 fusion.4
  116.6 1.7 add_convert_fusion.5
  118.3 1.5 fusion.288
  129.7 7.3 multiply_convert_fusion.7
  137.9 3.2 add_convert_fusion.4
  141.9 20.2 %all-gather.6 = bf16[1,1,64,1024]{3,2,1,0:T(8,128)(2,1)} all-gather(bf16[1,1,64,128]{3,2,1,0:T(8,128)(2,1)S(1)} %copy-done.88), channel_id=8, replica_groups=mesh['shards'=8,'context'=16] {'shards'}, dimensions={3}, use_global_device_ids=true | all-gather | bytes 147456 | tf_op jit(solution)/shard_map/all_gather | solution.py:206
  164.7 21.7 %all-gather.5 = bf16[1,1024,1,192]{1,3,2,0:T(8,128)(2,1)S(1)} all-gather(bf16[1,128,1,192]{1,3,2,0:T(8,128)(2,1)} %get-tuple-element.296), channel_id=7, replica_groups=mesh['shards'=8,'context'=16] {'shards'}, dimensions={1}, use_global_device_ids=true | all-gather | bytes 442368 | tf_op jit(solution)/shard_map/all_gather | solution.py:205
  186.3 1.4 fusion.286
  187.7 1.4 fusion.287
  189.1 28.7 %all-gather.8 = bf16[1,256,1024]{2,1,0:T(8,128)(2,1)} all-gather(bf16[1,256,128]{2,1,0:T(8,128)(2,1)} %get-tuple-element.292), channel_id=10, replica_groups=mesh['shards'=8,'context'=16] {'shards'}, dimensions={2}, use_global_device_ids=true | all-gather | bytes 589824 | tf_op jit(solution)/shard_map/all_gather | solution.py:208
  217.8 26.8 %all-gather.7 = bf16[1,1024,256]{2,1,0:T(8,128)(2,1)} all-gather(bf16[1,128,256]{2,1,0:T(8,128)(2,1)} %get-tuple-element.294), channel_id=9, replica_groups=mesh['shards'=8,'context'=16] {'shards'}, dimensions={1}, use_global_device_ids=true | all-gather | bytes 589824 | tf_op jit(solution)/shard_map/all_gather | solution.py:207
  244.6 4.3 fusion.45
  248.9 71.7 %all-reduce.11.cloned.1.call-done = bf16[2048,1024]{1,0:T(8,128)(2,1)} async-done(((bf16[2048,1024]{1,0:T(8,128)(2,1)}), bf16[2048,1024]{1,0:T(8,128)(2,1)}) %all-reduce.11.cloned.1.call-update) | async-done | bytes 4194320 | tf_op jit(solution)/shard_map/psum | solution.py:221
  320.7 5.2 fusion.275
  327.0 2.1 copy-done.2
  329.2 4.2 add_convert_fusion.3
  333.5 1.6 fusion.293
  357.2 1.5 bitcast_dynamic-update-slice_fusion.1
  360.1 6.5 multiply_convert_fusion.6
  366.6 2.6 convert_reduce_fusion.1
  370.2 3.4 add_convert_fusion.1
  375.5 1.6 fusion.122
  385.5 1.8 copy.44
  387.4 3.5 convolution_convert_fusion.4
  394.6 4.6 fusion.81
  399.2 2.1 copy.34
  401.3 123.4 %all-reduce.13.cloned.1.call-done = bf16[2048,1024]{1,0:T(8,128)(2,1)} async-done(((bf16[2048,1024]{1,0:T(8,128)(2,1)}), bf16[2048,1024]{1,0:T(8,128)(2,1)}) %all-reduce.13.cloned.1.call-update) | async-done | bytes 4194320 | tf_op jit(solution)/shard_map/psum | solution.py:302
  524.7 6.4 multiply_reduce_fusion.3
  531.8 7.4 fusion.273
  539.3 1.4 convolution_convert_fusion
  562.9 3.9 bitcast_dynamic-update-slice_fusion
  569.0 4.5 fusion.166
  575.9 4.7 convolution_convert_fusion.2
  580.6 6.7 add_convert_fusion.2
  587.4 5.5 convert_reduce_fusion.2
  592.9 2.2 convolution_convert_fusion.3
  596.7 3.5 add_convert_fusion
  605.2 32.8 %reduce-scatter.35.cloned.1.call-done = bf16[128,256]{1,0:T(8,128)(2,1)} async-done(((bf16[1024,256]{1,0:T(8,128)(2,1)}), bf16[128,256]{1,0:T(8,128)(2,1)}) %reduce-scatter.35.cloned.1.call-update) | async-done | bytes 65552
  639.3 3.2 convert_element_type.483
  646.6 30.2 %reduce-scatter.29.cloned.1.call-done = bf16[128,64]{1,0:T(8,128)(2,1)} async-done(((bf16[1024,64]{1,0:T(8,128)(2,1)}), bf16[128,64]{1,0:T(8,128)(2,1)}) %reduce-scatter.29.cloned.1.call-update) | async-done | bytes 16400
  678.3 38.0 %reduce-scatter.25.cloned.1.call-done = bf16[128,192]{1,0:T(8,128)(2,1)} async-done(((bf16[1024,192]{1,0:T(8,128)(2,1)}), bf16[128,192]{1,0:T(8,128)(2,1)}) %reduce-scatter.25.cloned.1.call-update) | async-done | bytes 49168
  718.0 37.0 %reduce-scatter.33.cloned.1.call-done = bf16[128,256]{1,0:T(8,128)(2,1)} async-done(((bf16[1024,256]{1,0:T(8,128)(2,1)}), bf16[128,256]{1,0:T(8,128)(2,1)}) %reduce-scatter.33.cloned.1.call-update) | async-done | bytes 65552
  756.7 37.1 %reduce-scatter.23.cloned.1.call-done = bf16[128,256]{1,0:T(8,128)(2,1)} async-done(((bf16[1024,256]{1,0:T(8,128)(2,1)}), bf16[128,256]{1,0:T(8,128)(2,1)}) %reduce-scatter.23.cloned.1.call-update) | async-done | bytes 65552 | tf_op jit(solution)/shard_map/reduce_scatter | solution.py:291
  793.8 38.9 %reduce-scatter.21.cloned.1.call-done = bf16[128,256]{1,0:T(8,128)(2,1)} async-done(((bf16[1024,256]{1,0:T(8,128)(2,1)}), bf16[128,256]{1,0:T(8,128)(2,1)}) %reduce-scatter.21.cloned.1.call-update) | async-done | bytes 65552 | tf_op jit(solution)/shard_map/reduce_scatter | solution.py:291
  832.7 1.6 maximum_convert_fusion
  834.2 208.1 %all-reduce.17.cloned.1.call-done = (bf16[2048,1024]{1,0:T(8,128)(2,1)}, bf16[2048,1024]{1,0:T(8,128)(2,1)}) async-done(((bf16[2048,1024]{1,0:T(8,128)(2,1)}, bf16[2048,1024]{1,0:T(8,128)(2,1)}), (bf16[2048,1024]{1,0:T(8,128)(2,1)}, bf16[2048,1024]{1,0:T(8,128)(2,1)})) %all-reduce.17.cloned.1.call-update) | async-done | bytes 8388624 | tf_op jit(solution)/shard_map/psum | solution.py:221
  1042.4 3.4 convert_element_type.496
  1047.1 5.1 fusion.52
  1052.3 2.2 dynamic-slice_reduce_fusion.1
  1055.8 1.9 fusion.160
  1057.7 136.0 %all-reduce.15.cloned.1.call-done = (f32[2,1024]{1,0:T(2,128)}, f32[2,1024]{1,0:T(2,128)}, f32[2,16,192]{2,1,0:T(8,128)}, f32[2,1024]{1,0:T(2,128)}, f32[2,4096]{1,0:T(2,128)}) async-done(((f32[2,1024]{1,0:T(2,128)}, f32[2,1024]{1,0:T(2,128)}, f32[2,16,192]{2,1,0:T(8,128)}, f32[2,1024]{1,0:T(2,128)}, f32[2,4096]{1,0:T(2,128)}), (f32[2,1024]{1,0:T(2,128)}, f32[2,1024]{1,0:T(2,128)}, f32[2,16,192]{2,1,0:T(8,128)}, ...) | async-done | bytes 81936 | tf_op jit(solution)/shard_map/psum | solution.py:311
  1197.6 1.4 copy.99
  1200.2 1.4 copy.101
  (494 shorter events, 109.6 us)
Async XLA Ops:
  7.2 104.5 %all-gather.13.cloned.1.call-start = ((), (), s32[]{:S(2)}) async-start(), calls=%async_computation.12 | async-start | bytes 4456448 | tf_op jit(solution)/shard_map/all_gather | solution.py:201
  7.9 236.7 %all-gather.15.cloned.1.call-start = ((), (), s32[]{:S(2)}) async-start(), calls=%async_computation.13 | async-start | bytes 4456448 | tf_op jit(solution)/shard_map/all_gather | solution.py:176
  8.7 312.0 %all-reduce.11.cloned.1.call-start = ((), (), s32[]{:S(2)}) async-start(), calls=%async_computation.8 | async-start | bytes 8388608 | tf_op jit(solution)/shard_map/psum | solution.py:221
  8.7 111.2 %copy-start.91 = (f32[8]{0:T(128)}, f32[8]{0:T(128)S(1)}, u32[]{:S(2)}) copy-start(f32[8]{0:T(128)S(1)} %negate_power_fusion) | copy-start | bytes 100
  8.7 112.2 %copy-start.136 = (s32[512]{0:T(512)}, s32[512]{0:T(512)S(1)}, u32[]{:S(2)}) copy-start(s32[512]{0:T(512)S(1)} %iota_add_fusion.2) | copy-start | bytes 6148
  8.8 113.4 %copy-start.134 = (s32[512]{0:T(512)}, s32[512]{0:T(512)S(1)}, u32[]{:S(2)}) copy-start(s32[512]{0:T(512)S(1)} %iota_add_fusion.1) | copy-start | bytes 6148
  8.8 115.2 %copy-start.132 = (s32[512]{0:T(512)}, s32[512]{0:T(512)S(1)}, u32[]{:S(2)}) copy-start(s32[512]{0:T(512)S(1)} %iota_add_fusion) | copy-start | bytes 6148
  10.2 106.4 %copy-start.94 = (f32[1,1024]{1,0:T(1,128)}, f32[1,1024]{1,0:T(1,128)S(1)}, u32[]{:S(2)}) copy-start(f32[1,1024]{1,0:T(1,128)S(1)} %get-tuple-element.305) | copy-start | bytes 12292
  38.3 89.9 %copy-start.48 = (bf16[1,1,64,1024]{3,2,1,0:T(8,128)(2,1)}, bf16[1,1,64,1024]{3,2,1,0:T(8,128)(2,1)S(1)}, u32[]{:S(2)}) copy-start(bf16[1,1,64,1024]{3,2,1,0:T(8,128)(2,1)S(1)} %all-gather.2) | copy-start | bytes 393220
  63.2 55.1 %copy-start.33 = (bf16[1,1024,1,192]{1,3,2,0:T(8,128)(2,1)}, bf16[1,1024,1,192]{1,3,2,0:T(8,128)(2,1)S(1)}, u32[]{:S(2)}) copy-start(bf16[1,1024,1,192]{1,3,2,0:T(8,128)(2,1)S(1)} %all-gather.1) | copy-start | bytes 1179652
  118.3 11.3 copy-start.19
  119.9 7.3 copy-start.29
  120.3 3.7 copy-start.62
  120.3 3.7 copy-start.64
  120.4 3.6 copy-start.56
  121.6 4.1 copy-start.15
  121.6 4.1 copy-start.124
  122.1 3.6 copy-start.126
  123.9 4.4 copy-start.66
  129.6 8.3 copy-start.39
  141.2 383.5 %all-reduce.13.cloned.1.call-start = ((), (), s32[]{:S(2)}) async-start(), calls=%async_computation.9 | async-start | bytes 8388608 | tf_op jit(solution)/shard_map/psum | solution.py:302
  329.2 4.3 copy-start.103
  333.4 26.6 %copy-start.22 = (bf16[2048,1024]{1,0:T(8,128)(2,1)}, bf16[2048,1024]{1,0:T(8,128)(2,1)S(1)}, u32[]{:S(2)}) copy-start(bf16[2048,1024]{1,0:T(8,128)(2,1)S(1)} %get-tuple-element.275) | copy-start | bytes 12582916
  335.0 14.1 %copy-start.31 = (bf16[2048,1,192]{0,2,1:T(8,128)(2,1)}, bf16[2048,1,192]{0,2,1:T(8,128)(2,1)S(1)}, u32[]{:S(2)}) copy-start(bf16[2048,1,192]{0,2,1:T(8,128)(2,1)S(1)} %get-tuple-element.323) | copy-start | bytes 2359300
  339.4 4.1 copy-start.120
  339.4 6.3 copy-start.7
  348.4 8.8 copy-start.5
  352.7 6.1 copy-start.36
  360.1 6.6 copy-start.9
  360.1 6.6 copy-start.41
  373.7 229.7 %reduce-scatter.31.cloned.1.call-start = ((), (), s32[]{:S(2)}) async-start(), calls=%async_computation.17 | async-start | bytes 294912
  377.1 5.2 copy-start.74
  387.4 216.9 %reduce-scatter.27.cloned.1.call-start = ((), (), s32[]{:S(2)}) async-start(), calls=%async_computation.15 | async-start | bytes 589824
  392.0 246.1 %reduce-scatter.35.cloned.1.call-start = ((), (), s32[]{:S(2)}) async-start(), calls=%async_computation.19 | async-start | bytes 589824
  394.6 130.1 %copy-start.90 = (f32[1,1024]{1,0:T(1,128)S(1)}, f32[1,1024]{1,0:T(1,128)}, u32[]{:S(2)}) copy-start(f32[1,1024]{1,0:T(1,128)} %get-tuple-element.304) | copy-start | bytes 12292
  401.3 275.5 %reduce-scatter.29.cloned.1.call-start = ((), (), s32[]{:S(2)}) async-start(), calls=%async_computation.16 | async-start | bytes 294912
  524.7 6.4 copy-start.11
  524.7 7.1 copy-start.14
  531.8 7.5 copy-start.49
  539.3 21.2 %copy-start.12 = (bf16[2048,1024]{1,0:T(8,128)(2,1)}, bf16[2048,1024]{1,0:T(8,128)(2,1)S(1)}, u32[]{:S(2)}) copy-start(bf16[2048,1024]{1,0:T(8,128)(2,1)S(1)} %get-tuple-element.271) | copy-start | bytes 12582916
  556.0 4.5 copy-start.67
  556.0 4.5 copy-start.69
  556.1 4.5 copy-start.71
  556.1 4.5 copy-start.73
  562.6 153.7 %reduce-scatter.25.cloned.1.call-start = ((), (), s32[]{:S(2)}) async-start(), calls=%async_computation.14 | async-start | bytes 589824
  562.9 3.9 copy-start.20
  568.9 4.7 copy-start.51
  568.9 186.2 %reduce-scatter.33.cloned.1.call-start = ((), (), s32[]{:S(2)}) async-start(), calls=%async_computation.18 | async-start | bytes 589824
  569.0 4.6 copy-start.13
  575.8 4.8 copy-start.42
  575.8 4.8 copy-start.52
  575.9 217.9 %reduce-scatter.23.cloned.1.call-start = ((), (), s32[]{:S(2)}) async-start(), calls=%async_computation.11 | async-start | bytes 589824 | tf_op jit(solution)/shard_map/reduce_scatter | solution.py:291
  580.6 6.8 copy-start.40
  587.3 245.3 %reduce-scatter.21.cloned.1.call-start = ((), (), s32[]{:S(2)}) async-start(), calls=%async_computation.10 | async-start | bytes 589824 | tf_op jit(solution)/shard_map/reduce_scatter | solution.py:291
  587.4 5.5 copy-start.21
  595.1 447.3 %all-reduce.17.cloned.1.call-start = ((), (), s32[]{:S(2)}) async-start(), calls=%async_computation.21 | async-start | bytes 16777216 | tf_op jit(solution)/shard_map/psum | solution.py:221
  600.2 38.8 %copy-start.59 = (bf16[2048,1,192]{0,2,1:T(8,128)(2,1)S(1)}, bf16[2048,1,192]{0,2,1:T(8,128)(2,1)}, u32[]{:S(2)}) copy-start(bf16[2048,1,192]{0,2,1:T(8,128)(2,1)} %get-tuple-element.251) | copy-start | bytes 2359300
  600.2 38.8 %copy-start.55 = (bf16[2048,1,64]{0,2,1:T(8,128)(2,1)S(1)}, bf16[2048,1,64]{0,2,1:T(8,128)(2,1)}, u32[]{:S(2)}) copy-start(bf16[2048,1,64]{0,2,1:T(8,128)(2,1)} %get-tuple-element.353) | copy-start | bytes 786436
  600.2 593.4 %all-reduce.15.cloned.1.call-start = ((), (), s32[]{:S(2)}) async-start(), calls=%async_computation.20 | async-start | bytes 180224 | tf_op jit(solution)/shard_map/psum | solution.py:311
  1042.4 4.7 copy-start.26
  1042.4 4.7 copy-start.85
  1042.4 4.7 copy-start.95
  1052.2 3.6 copy-start.100
  1052.2 3.6 copy-start.101
  (91 other events, 161.7 us)
Sparse Core Ops, SparseCore 0:
  10.4 65.4 all-gather.12
  78.3 59.1 all-gather.14
  141.3 179.2 all-reduce.10
  373.8 150.8 all-reduce.12
  526.9 33.6 reduce-scatter.30
  562.9 36.3 reduce-scatter.26
  601.6 36.3 reduce-scatter.34
  641.1 35.6 reduce-scatter.28
  679.7 36.5 reduce-scatter.24
  718.7 36.3 reduce-scatter.32
  757.4 36.3 reduce-scatter.22
  796.1 36.4 reduce-scatter.20
  835.2 207.1 all-reduce.16
  1055.9 137.7 all-reduce.14
where the time goes:
time: 1220 us; the launch traced here: 1210 us
  waiting for transfers between devices  755 us (62%)
  blocking collectives  188 us (15%)
  matrix products  109 us (9%)
  other arithmetic  78.8 us (6%)
  local copies, waits for them, and re-layouts  60 us (5%)
  between operations  16.6 us (1%)
    psum x2, waiting for transfers between devices, on_device(): lax.psum(branch_rows(mixed_low, active_low, full_weights[1], full_weights...  280 us
    unnamed x20, waiting for transfers between devices  140 us
    psum x1, waiting for transfers between devices, on_device(): lax.psum((jnp.stack(gain_grads), jnp.stack(shift_grads), jnp.stack(qkv_bi...  136 us
    psum x1, waiting for transfers between devices, on_device(): lax.psum(normed_grad_rows(grad_proj, grad_hidden, w_qkv, w_up).astype(jnp...  123 us
    reduce_scatter x2, waiting for transfers between devices, on_device(): lax.psum_scatter(grad_w_up.astype(jnp.bfloat16), 'shards', scatter_dimens...  76 us
    all_gather x2, blocking collectives, on_device(): lax.all_gather(fc1_weight[layer_index], 'shards', axis=0, tiled=True)  51.9 us
    all_gather x2, blocking collectives, on_device(): lax.all_gather(fc2_weight[layer_index], 'shards', axis=1, tiled=True)  51.6 us
    all_gather x2, blocking collectives, on_device(): lax.all_gather(qkv_weight[layer_index], 'shards', axis=0, tiled=True)  43.5 us
  transfers between devices with their start and end apart: 14, of which 10 were waited for; matrix products, arithmetic and copies ran while one was open for 13% of the time, Pallas kernels for 0%

commit v1 on v0

v1 whole, which is shorter than its diff:
```python
import jax
import jax.numpy as jnp
import numpy as np
from jax import lax
from jax.experimental import pallas as pl
from jax.experimental.pallas import tpu as pltpu
from jax.sharding import PartitionSpec as P

HD = 64
ROT = 16
LAYERS = 2
EPSILON = 1e-05
MASKED = -1e30
MESH = pl.DeviceIdType.MESH
F32 = jnp.float32
BF16 = jnp.bfloat16
VMEM_LIMIT = 127 * 512 * 1024
IN_ROWS = slice(0, 448)
OUT_ROWS = slice(448, 768)
ORDER = (2, 1, -1, 0)
ARRIVAL = (0, -1, 1, 2)


def dot(lhs, rhs, lhs_axis=1, rhs_axis=0):
    return lax.dot_general(
        lhs, rhs, (((lhs_axis,), (rhs_axis,)), ((), ())), preferred_element_type=F32
    )


def step(index, by):
    return lax.rem(index + by + 4, 4)


class Here:
    def __init__(self):
        shard = lax.axis_index("shards")
        place = lax.axis_index("context")
        self.x, self.zl = lax.div(shard, 2), lax.rem(shard, 2)
        self.y, self.zh = lax.div(place, 4), lax.rem(lax.div(place, 2), 2)
        self.core = lax.rem(place, 2)
        self.z = self.zh * 2 + self.zl

    def at(self, dx=0, dy=0, dz=0, other_core=False):
        x, y, z = (lax.rem(v + d + 4, 4) for v, d in ((self.x, dx), (self.y, dy), (self.z, dz)))
        core = 1 - self.core if other_core else self.core
        return (x * 2 + lax.rem(z, 2), y * 4 + lax.div(z, 2) * 2 + core)


class Mail:
    def __init__(self, send, receive, like, device):
        self.send, self.receive, self.like, self.device = send, receive, like, device
        self.forms, self.gone = [], set()

    def reserve(self, shape, dtype):
        self.forms.append((shape, dtype))
        return len(self.forms) - 1

    def post(self, source, target, device, k=None):
        if k is None:
            k = self.reserve(source.shape, source.dtype)
        pltpu.make_async_remote_copy(
            src_ref=source,
            dst_ref=target,
            send_sem=self.send.at[k],
            recv_sem=self.receive.at[k],
            device_id=device,
            device_id_type=MESH,
        ).start()
        return k

    def sent(self, k):
        ref = self.like(*self.forms[k])
        return pltpu.make_async_remote_copy(
            src_ref=ref,
            dst_ref=ref,
            send_sem=self.send.at[k],
            recv_sem=self.receive.at[k],
            device_id=self.device,
            device_id_type=MESH,
        )

    def take(self, *posts):
        for k in posts:
            self.sent(k).wait_recv()

    def finish(self, count=None):
        for k in range(len(self.forms) if count is None else count):
            if k not in self.gone:
                self.sent(k).wait_send()
                self.gone.add(k)


def at_step(n, actions):
    for m, action in enumerate(actions):
        if action is not None:
            pl.when(n == m)(action)


def tell(semaphore, devices):
    for device in devices:
        pl.semaphore_signal(semaphore, inc=1, device_id=device, device_id_type=MESH)


class RingGather:
    def __init__(self, mail, place, me, right, left):
        self.mail, self.place, self.me, self.right, self.left = mail, place, me, right, left

    def post(self, half, to, source=None):
        ref = self.place(self.me if source is None else source, half)
        return self.mail.post(ref, ref, to)

    def start(self):
        self.from_left = [self.post(0, self.right), None]
        self.from_right = [None, self.post(1, self.left)]
        self.from_left[1] = self.post(1, self.right)
        self.from_right[0] = self.post(0, self.left)

    def start_half(self, half):
        if half == 0:
            self.from_left, self.from_right = [self.post(0, self.right), None], [None, None]
        else:
            self.from_right[1] = self.post(1, self.left)
            self.from_left[1] = self.post(1, self.right)
            self.from_right[0] = self.post(0, self.left)

    def relay(self):
        self.relay_half(0)
        self.relay_half(1)

    def relay_half(self, half):
        if half == 0:
            self.mail.take(self.from_left[0])
            self.opposite = [self.post(0, self.right, step(self.me, -1))]
        else:
            self.mail.take(self.from_right[1])
            self.opposite.append(self.post(1, self.left, step(self.me, 1)))

    def near(self):
        self.mail.take(self.from_left[1], self.from_right[0])

    def far(self):
        self.mail.take(*self.opposite)


class RingReduce:
    def __init__(self, mail, part, slots, me, right, left):
        self.mail, self.part, self.slots = mail, part, slots
        self.me, self.right, self.left = me, right, left

    def start_far(self, ready=lambda half: None):
        far = step(self.me, 2)
        self.relays = []
        for half, to in ((0, self.right), (1, self.left)):
            ready(half)
            self.relays.append(self.mail.post(self.part(far, half), self.slots(half), to))

    def start_right(self):
        self.arrivals = [self.mail.post(self.part(step(self.me, 1), 1), self.slots(2), self.right)]

    def start_left(self):
        self.arrivals.append(self.mail.post(self.part(step(self.me, -1), 0), self.slots(3), self.left))

    def start_near(self):
        self.start_right()
        self.start_left()

    def relay_half(self, half):
        near, to = ((step(self.me, 1), self.right), (step(self.me, -1), self.left))[half]
        self.mail.take(self.relays[half])
        ref = self.part(near, half)
        ref[...] = (ref[...].astype(F32) + self.slots(half)[...].astype(F32)).astype(BF16)
        self.arrivals.append(self.mail.post(ref, self.slots(4 + half), to))

    def relay(self):
        self.relay_half(0)
        self.relay_half(1)

    def total(self, half, own=None):
        first, second = ((4, 2), (3, 1)) if half == 0 else ((2, 0), (5, 3))
        self.mail.take(self.arrivals[first[1]], self.arrivals[second[1]])
        own = self.part(self.me, half)[...].astype(F32) if own is None else own
        return own + self.slots(first[0])[...].astype(F32) + self.slots(second[0])[...].astype(F32)


class RowsGather:
    def __init__(self, here, mail, buf):
        self.here, self.mail, self.buf = here, mail, buf
        self.partner = here.at(other_core=True)
        self.relayed = self.nearby = False
        self.ring = RingGather(mail, self.place, here.y, here.at(dy=1), here.at(dy=-1))

    def place(self, i, half):
        return self.buf.at[i, self.here.core, pl.ds(half * 64, 64)]

    def share(self, d, half):
        ref = self.place(step(self.here.y, d), half)
        return self.mail.post(ref, ref, self.partner)

    def start_half(self, half):
        self.ring.start_half(half)
        if half == 0:
            self.shared = []
        self.shared.append(self.share(0, half))

    def start(self):
        self.start_half(0)
        self.start_half(1)

    def relay(self):
        self.ring.relay_half(0)
        self.shared.append(self.share(-1, 0))
        self.ring.relay_half(1)
        self.shared.append(self.share(1, 1))
        self.relayed = True

    def near(self):
        if not self.relayed:
            self.relay()
        self.nearby = True
        self.mail.take(self.ring.from_left[1])
        self.shared.append(self.share(-1, 1))
        self.mail.take(self.ring.from_right[0])
        self.shared.append(self.share(1, 0))

    def far(self):
        for half in range(2):
            self.mail.take(self.ring.opposite[half])
            self.shared.append(self.share(2, half))

    def ready(self, d):
        first = {0: (0, 1), -1: (2, 4), 1: (3, 5), 2: (6, 7)}[d]
        self.mail.take(*(self.shared[k] for k in first))


class RowsReduce:
    def __init__(self, here, mail, part, from_partner, summed, slots):
        self.here, self.mail = here, mail
        self.part, self.from_partner, self.summed = part, from_partner, summed
        self.partner = here.at(other_core=True)
        self.halves = {2: (0, 1), 1: (1, 0), -1: (0, 1), 0: (0, 1)}
        self.ring = RingReduce(
            mail,
            lambda i, half: summed.at[i, pl.ds(half * 64, 64)],
            lambda k: slots.at[k],
            here.y,
            here.at(dy=1),
            here.at(dy=-1),
        )
        self.posts = {d: [mail.reserve((64, 1024), BF16) for _ in range(2)] for d in ORDER}

    def chunk(self, d):
        i = step(self.here.y, d)
        for half in self.halves[d]:
            rows = pl.ds(half * 64, 64)
            self.mail.post(
                self.part.at[i, 1 - self.here.core, rows],
                self.from_partner.at[i, rows],
                self.partner,
                self.posts[d][half],
            )

    def pair(self, d, half):
        i, rows = step(self.here.y, d), pl.ds(half * 64, 64)
        self.mail.take(self.posts[d][half])
        return self.part[i, self.here.core, rows].astype(F32) + self.from_partner[i, rows].astype(F32)

    def add(self, d, half):
        self.summed[step(self.here.y, d), pl.ds(half * 64, 64)] = self.pair(d, half).astype(BF16)

    def send_far(self):
        self.ring.start_far(lambda half: self.add(2, half))

    def send_right(self):
        self.add(1, 1)
        self.ring.start_right()
        self.add(1, 0)

    def send_left(self):
        self.add(-1, 0)
        self.ring.start_left()
        self.ring.relay_half(0)
        self.add(-1, 1)
        self.ring.relay_half(1)

    def totals(self):
        for half in range(2):
            yield half, self.ring.total(half, self.pair(0, half))


def row_halves(begin, first, second):
    starts = (begin, begin + first, begin + 2 * first, begin + 2 * first + second)
    return lambda part, half: pl.ds(starts[2 * part + half], (first, second)[part])


def split(j):
    return lax.div(j, 2), lax.rem(j, 2)


class WeightGather:
    def __init__(self, here, mail, buf, begin, first, second):
        along_x = (here.x, here.at(dx=1), here.at(dx=-1))
        along_z = (here.z, here.at(dz=1), here.at(dz=-1))
        rows = row_halves(begin, first, second)
        self.rings = (
            RingGather(mail, lambda i, h: buf.at[i, here.zh, here.zl, rows(0, h)], *along_x),
            RingGather(mail, lambda j, h: buf.at[(here.x, *split(j), rows(1, h))], *along_z),
            RingGather(mail, lambda j, h: buf.at[(slice(None), *split(j), rows(0, h))], *along_z),
            RingGather(mail, lambda i, h: buf.at[i, :, :, rows(1, h)], *along_x),
        )

    def start(self):
        self.rings[0].start()
        self.rings[1].start()

    def relay(self):
        self.rings[0].relay()
        self.rings[1].relay()

    def turn(self, parts=(0, 1)):
        for part in parts:
            self.rings[part].near()
            self.rings[part].far()
            self.rings[part + 2].start()

    def late(self, parts=(0, 1)):
        for part in parts:
            self.rings[part + 2].relay()

    def end(self):
        for ring in self.rings[2:]:
            ring.near()
            ring.far()


class WeightReduce:
    def __init__(self, here, mail, part, begin, first, second, slots):
        along_x = (here.x, here.at(dx=1), here.at(dx=-1))
        along_z = (here.z, here.at(dz=1), here.at(dz=-1))
        slots_z, slots_x, slots_third, slots_fourth = slots
        rows = row_halves(begin, first, second)
        self.rows, self.x, self.z = rows, here.x, (here.zh, here.zl)
        self.first = RingReduce(
            mail, lambda j, k: part.at[(slice(None), *split(j), rows(0, k))], lambda k: slots_z.at[k], *along_z
        )
        self.second = RingReduce(
            mail, lambda i, k: part.at[i, :, :, rows(1, k)], lambda k: slots_x.at[k], *along_x
        )
        self.third = RingReduce(
            mail,
            lambda i, k: part.at[i, here.zh, here.zl, rows(0, k)],
            lambda k: slots_third.at[k],
            *along_x,
        )
        self.fourth = RingReduce(
            mail,
            lambda j, k: part.at[(here.x, *split(j), rows(1, k))],
            lambda k: slots_fourth.at[k],
            *along_z,
        )
        self.part = part

    def start(self):
        for ring in (self.first, self.second):
            ring.start_far()
        for ring in (self.first, self.second):
            ring.start_near()

    def relay(self):
        for ring in (self.first, self.second):
            ring.relay()

    def turn(self):
        for half in range(2):
            self.part[(slice(None), *self.z, self.rows(0, half))] = self.first.total(half).astype(BF16)
            self.part[self.x, :, :, self.rows(1, half)] = self.second.total(half).astype(BF16)
        for ring in (self.third, self.fourth):
            ring.start_far()
        for ring in (self.third, self.fourth):
            ring.start_near()

    def late(self):
        for ring in (self.third, self.fourth):
            ring.relay()

    def end(self, out):
        for half in range(2):
            out[self.rows(0, half)] = self.third.total(half)
            out[self.rows(1, half)] = self.fourth.total(half)


def reduce_slots(name, first, second):
    return {
        name + "_z": ((6, 4, first, 128), BF16),
        name + "_x": ((6, 2, 2, second, 128), BF16),
        name + "_third": ((6, first, 128), BF16),
        name + "_fourth": ((6, second, 128), BF16),
    }


def ways(k):
    if k < 2:
        return ((0, 128, 1), (128, 128, -1))
    return ((0, 64, 1), (128, 64, -1), (64, 64, 1), (192, 64, -1))


class Swap:
    def __init__(self, here, mail, relays):
        self.here, self.mail, self.relays = here, mail, relays
        self.hops, self.arrivals = (
            [[mail.reserve((rows, 256), BF16) for _, rows, _ in ways(k)] for k in range(4)] for _ in range(2)
        )

    def post(self, k, source):
        for side, (begin, count, d) in enumerate(ways(k)):
            rows = pl.ds(begin, count)
            self.mail.post(
                source.at[rows], self.relays.at[k, rows], self.here.at(dz=d), self.hops[k][side]
            )

    def relay(self, k, target):
        for side, (begin, count, d) in enumerate(ways(k)):
            rows = pl.ds(begin, count)
            self.mail.take(self.hops[k][side])
            place = target(lax.div(step(self.here.z, -d), 2))
            self.mail.post(
                self.relays.at[k, rows], place.at[rows], self.here.at(dz=d), self.arrivals[k][side]
            )

    def arrived(self, k):
        self.mail.take(*self.arrivals[k])


def column_sum(value):
    return jnp.sum(value.reshape(-1, 8, value.shape[1]), axis=0)


def column_max(value):
    return jnp.max(value.reshape(-1, 8, value.shape[1]), axis=0)


def turn(section, cosine, sine):
    front, back = section[0:8], section[8:16]
    return jnp.concatenate(
        [front * cosine - back * sine, back * cosine + front * sine, section[ROT:]], axis=0
    )


def two_blocks(first, second):
    zero = jnp.zeros_like(first)
    return jnp.concatenate(
        [jnp.concatenate([first, zero], axis=1), jnp.concatenate([zero, second], axis=1)], axis=0
    )


def vector_row(kind, layer):
    return 8 * (kind if kind < 2 and layer == 0 else (2 + kind if layer else 5))


class Program:
    def __init__(self, refs):
        self.__dict__.update(refs)
        self.here = Here()
        self.near_x = [self.here.at(dx=d) for d in (1, -1)]
        self.near_y = [self.here.at(dy=d) for d in (1, -1)]
        self.near_z = [self.here.at(dz=d) for d in (1, -1)]
        self.partner = self.here.at(other_core=True)
        self.far = [self.here.at(dx=2), self.here.at(dy=2), self.here.at(dz=2)]
        self.reduced = 0
        self.mail = Mail(self.send, self.receive, self.like, self.partner)


    def like(self, shape, dtype):
        if dtype == F32:
            return self.vectors.at[0, 0 : shape[0]] if shape[0] <= 64 else self.vector_whole.at[0, 0 : shape[0]]
        if shape[-1] == 1024:
            return self.part.at[0, 0, 0 : shape[0]]
        if shape[-1] == 256:
            return self.relays.at[0, 0, 0 : shape[0]]
        rows = slice(0, shape[-2])
        return {
            2: lambda: self.weights.at[0, 0, 0, 0, rows],
            3: lambda: self.weights.at[0, :, 0, 0, rows],
            4: lambda: self.weights.at[0, 0, :, :, rows],
        }[len(shape)]()

    def ordered(self, k):
        return lax.rem(self.here.y + jnp.where(k == 0, 2, jnp.where(k == 1, 1, jnp.where(k == 2, 3, 0))), 4)

    def arriving(self, n):
        return lax.rem(self.here.y + jnp.where(n == 0, 0, jnp.where(n == 1, 3, jnp.where(n == 2, 1, 2))), 4)

    def weight(self, layer, rows):
        return jnp.concatenate(
            [
                jnp.concatenate(
                    [self.weights[layer, x, zh, half, rows] for half in range(2) for x in range(4)], axis=1
                )
                for zh in range(2)
            ],
            axis=0,
        )

    def chunk(self, buf, i):
        return buf[i].reshape(256, 1024)

    def chunk_pair(self, buf, pair):
        return buf[pl.ds(pair * 2, 2)].reshape(512, 1024)

    def arrange(self, ref):
        return jnp.concatenate(
            [ref[:, (x * 2 + zl) * 128 : (x * 2 + zl) * 128 + 128] for zl in range(2) for x in range(4)],
            axis=1,
        )

    def restore(self, ref, value):
        for zl in range(2):
            for x in range(4):
                ref[:, (x * 2 + zl) * 128 : (x * 2 + zl) * 128 + 128] = value[
                    :, (zl * 4 + x) * 128 : (zl * 4 + x) * 128 + 128
                ]

    def keep_sum(self, kind, layer, value):
        for zl in range(2):
            for x in range(4):
                row = vector_row(kind, layer) + x * 2 + zl
                self.vectors[0, row : row + 1, :] = value[:, (zl * 4 + x) * 128 : (zl * 4 + x) * 128 + 128]


    def norm(self, layer, half):
        rows = slice(half * 64, half * 64 + 64)
        rows_in = self.stream[rows]
        centered = rows_in - jnp.mean(rows_in, axis=-1, keepdims=True)
        variance = jnp.mean(centered * centered, axis=-1, keepdims=True)
        inverse = lax.rsqrt(variance + EPSILON)
        normal = centered * inverse
        self.normal[layer, rows] = normal
        self.inverse[layer, rows] = jnp.broadcast_to(inverse, (64, 128))
        normed = normal * self.vector(self.gain, layer) + self.vector(self.shift, layer)
        self.rows[layer, self.here.y, self.here.core, rows] = normed.astype(BF16)

    def vector(self, ref, layer):
        return self.arrange(ref.at[layer : layer + 1])

    def prepare(self, layer):
        here = self.here
        own = self.weights.at[layer, here.x, here.zh, here.zl]
        own[0:192] = self.qkv_weight[layer]
        own[192:448] = self.fc1_weight[layer].T
        own[448:512] = self.out_weight[layer]
        own[512:768] = self.fc2_weight[layer]

    def prepare_bias(self, layer):
        here = self.here
        for zh in range(2):
            head = here.y * 4 + zh * 2 + here.core
            first = self.qkv_bias[layer, pl.ds(head, 1), :]
            second = self.fc1_bias[layer : layer + 1, pl.ds(pl.multiple_of(head * 256, 256), 256)]
            self.bias[zh, 0:192] = jnp.broadcast_to(first, (8, 192)).T
            self.bias[zh, 192:448] = jnp.broadcast_to(second, (8, 256)).T

    def project(self, layer, i):
        cosine, sine = self.angles[self.here.zh, 0, i], self.angles[self.here.zh, 1, i]
        keys, values, queries = [], [], []
        whole = dot(self.weight(layer, slice(0, 192)), self.chunk(self.rows.at[layer], i), 1, 1)
        for head in range(2):
            out = whole[head * 192 : head * 192 + 192] + self.bias[head, 0:192, 0:1]
            queries.append((turn(out[0:64], cosine, sine) * HD**-0.5).astype(BF16))
            keys.append(turn(out[64:128], cosine, sine).astype(BF16))
            values.append(out[128:192].astype(BF16))
        self.queries[layer, i] = two_blocks(*queries)
        both = jnp.concatenate(keys + values, axis=0)
        here = i * 2 + self.here.zh
        self.across[layer, here] = both
        self.along[layer, here] = both.T

    def units(self, layer, pair):
        whole = dot(self.weight(layer, slice(192, 448)), self.chunk_pair(self.rows.at[layer], pair), 1, 1)
        for place in range(2):
            i = pair * 2 + place
            for zh in range(2):
                hidden = whole[zh * 256 : zh * 256 + 256, place * 256 : place * 256 + 256]
                hidden = hidden + self.bias[zh, 192:448, 0:1]
                cumulative = 0.5 + 0.5 * lax.erf(hidden * 0.5**0.5)
                slope = cumulative + hidden * (jnp.exp(-0.5 * hidden * hidden) * (2.0 * np.pi) ** -0.5)
                self.slope[layer, i, zh] = slope.astype(BF16)
                self.into_out[layer, i, zh, 64:320] = (hidden * cumulative).astype(BF16)

    def prepare_mask(self):
        key = lax.broadcasted_iota(jnp.int32, (512, 256), 0)
        query = lax.broadcasted_iota(jnp.int32, (512, 256), 1)
        self.mask[0] = jnp.zeros((512, 256), F32)
        self.mask[1] = jnp.where(key <= query + self.here.zh * 256, 0.0, MASKED)

    def score(self, layer, i, pair):
        keys = self.along[layer, pl.ds(pair * 2, 2), :, 0:128].reshape(512, 128)
        mask = self.mask[jnp.where(i == pair, 1, 0)]
        return dot(keys, self.queries[layer, i]) + jnp.concatenate([mask, mask], axis=1)

    def clear_attention(self):
        self.peaks[...] = jnp.full((4, 8, 512), MASKED, F32)
        self.totals[...] = jnp.zeros((4, 8, 512), F32)
        self.mixed[...] = jnp.zeros((4, 128, 256), F32)

    def attend(self, layer, i, pair):
        scores = self.score(layer, i, pair)
        before = self.peaks[i, 0:1]
        peak = jnp.maximum(before, jnp.max(column_max(scores), axis=0, keepdims=True))
        shrink = jnp.exp(before - peak)
        terms = jnp.exp(scores - peak)
        self.peaks[i] = jnp.broadcast_to(peak, (8, 512))
        self.totals[i] = self.totals[i] * shrink + column_sum(terms)
        low = terms.astype(BF16)
        for head in range(2):
            rows = slice(128 + head * 64, 192 + head * 64)
            at = slice(head * 256, head * 256 + 256)
            values = jnp.concatenate(
                [self.across[layer, pair * 2, rows], self.across[layer, pair * 2 + 1, rows]], axis=1
            )
            mine = slice(head * 64, head * 64 + 64)
            self.mixed[i, mine] = self.mixed[i, mine] * shrink[:, at] + dot(values, low[:, at])

    def attended(self, layer, i):
        total = jnp.sum(self.totals[i], axis=0, keepdims=True)
        for head in range(2):
            self.into_out[layer, i, head, 0:64] = (
                self.mixed[i, head * 64 : head * 64 + 64] / total[:, head * 256 : head * 256 + 256]
            ).astype(BF16)
        self.logs[layer, i] = jnp.broadcast_to(self.peaks[i, 0:1] + jnp.log(total), (8, 512))

    def each_unit(self, k, work):
        mine = self.ordered(k)

        def one(later, _):
            other = self.ordered(later)
            work(jnp.maximum(mine, other), jnp.minimum(mine, other), later)
            return 0

        lax.fori_loop(k, 4, one, 0)

    def spread_rows(self, i, units, layer, rows):
        value = dot(units.T, self.weight(layer, rows)).astype(BF16)
        self.part[i] = value.reshape(2, 128, 1024)

    def rows_reduce(self):
        self.mail.finish(self.reduced)
        return RowsReduce(self.here, self.mail, self.part, self.from_partner, self.summed, self.slots)

    def project_all(self, layer, gather, between):
        here = self.here
        self.mail.finish(self.reduced)
        self.swap = swap = Swap(here, self.mail, self.relays.at[layer])

        def near():
            if not gather.nearby:
                gather.near()

        def post(n):
            def run():
                swap.post(n, self.across.at[layer, step(here.y, ARRIVAL[n]) * 2 + here.zh])
                between[n]()

            return run

        def one(n, _):
            at_step(n, [None, near, None, gather.far])
            at_step(n, [lambda d=d: gather.ready(d) for d in ARRIVAL])
            self.project(layer, self.arriving(n))
            at_step(n, [post(m) for m in range(4)])
            return 0

        lax.fori_loop(0, 4, one, 0)

    def swap_relay(self, layer, n):
        i = step(self.here.y, ARRIVAL[n])
        self.swap.relay(n, lambda zh: self.across.at[layer, i * 2 + zh])

    def swapped(self, layer):
        def one(n, _):
            at_step(n, [lambda m=m: self.swap.arrived(m) for m in range(4)])
            other = self.arriving(n) * 2 + 1 - self.here.zh
            self.along[layer, other] = self.across[layer, other].T
            return 0

        lax.fori_loop(0, 4, one, 0)

    def mix(self, layer, hooks):
        reduce = self.rows_reduce()
        due = {(1, 3): reduce.send_far, (2, 3): reduce.send_right, (3, 3): reduce.send_left}

        def one(k, _):
            def unit(i, pair, later):
                self.attend(layer, i, pair)
                for table in (due, hooks):
                    for (first, second), action in table.items():
                        pl.when(jnp.logical_and(k == first, later == second))(action)

            self.each_unit(k, unit)
            i = self.ordered(k)
            self.attended(layer, i)
            self.spread_rows(i, self.into_out[layer, i].reshape(640, 256), layer, OUT_ROWS)
            at_step(k, [lambda d=d: reduce.chunk(d) for d in ORDER])
            return 0

        lax.fori_loop(0, 4, one, 0)
        return reduce


    def grads_of_pair(self, layer, pair):
        whole = dot(self.weight(layer, OUT_ROWS), self.chunk_pair(self.grad_rows.at[layer], pair), 1, 1)
        unit_grads = []
        for place in range(2):
            at = slice(place * 256, place * 256 + 256)
            self.mixed_grads[pair * 2 + place] = two_blocks(
                *(whole[zh * 320 : zh * 320 + 64, at].astype(BF16) for zh in range(2))
            )
            unit_grads.append([whole[zh * 320 + 64 : zh * 320 + 320, at] for zh in range(2)])
        return unit_grads

    def slope_of_chunk(self, layer, i, unit_grads):
        deltas = []
        for zh in range(2):
            both = self.mixed_grads[i, zh * 64 : zh * 64 + 64, zh * 256 : zh * 256 + 256].astype(F32)
            both = both * self.into_out[layer, i, zh, 0:64].astype(F32)
            deltas.append(jnp.sum(both, axis=0, keepdims=True))
            self.into_in[i, zh, 192:448] = (
                unit_grads[zh] * self.slope[layer, i, zh].astype(F32)
            ).astype(BF16)
        self.delta[i] = jnp.broadcast_to(jnp.concatenate(deltas, axis=1), (8, 512))
        self.mixed_grads_along[i] = self.mixed_grads[i].T
        self.queries_along[i] = self.queries[layer, i].T

    def grads_ahead(self, layer, pair):
        for place, unit_grads in enumerate(self.grads_of_pair(layer, pair)):
            for zh in range(2):
                self.into_in[pair * 2 + place, zh, 192:448] = unit_grads[zh].astype(BF16)

    def slope_after(self, layer, i):
        self.slope_of_chunk(layer, i, [self.into_in[i, zh, 192:448].astype(F32) for zh in range(2)])

    def grads_now(self, layer, pair):
        for place, unit_grads in enumerate(self.grads_of_pair(layer, pair)):
            self.slope_of_chunk(layer, pair * 2 + place, unit_grads)

    def weight_grads(self, layer, units, buf, rows):
        lhs = jnp.concatenate([units(zh) for zh in range(2)], axis=0)
        count = rows.stop - rows.start
        value = dot(lhs, buf[layer].reshape(1024, 1024)).astype(BF16)
        for zh in range(2):
            for half in range(2):
                for x in range(4):
                    self.weight_part[layer, x, zh, half, rows] = value[
                        zh * count : zh * count + count, half * 512 + x * 128 : half * 512 + x * 128 + 128
                    ]

    def clear_grads(self):
        def one(i, _):
            self.pair_grads[i] = jnp.zeros((512, 256), F32)
            self.grad_queries[i] = jnp.zeros((128, 256), F32)
            return 0

        lax.fori_loop(0, 4, one, 0)

    def attend_back(self, layer, i, pair):
        values = self.along[layer, pl.ds(pair * 2, 2), :, 128:256].reshape(512, 128)
        scores = self.score(layer, i, pair)
        probs = jnp.exp(scores - self.logs[layer, i, 0:1])
        grad_probs = dot(values, self.mixed_grads[i])
        grad_scores = (probs * (grad_probs - self.delta[i, 0:1])).astype(BF16)
        self.pair_grads[pair, :, 128:256] += dot(probs.astype(BF16), self.mixed_grads_along[i])
        self.pair_grads[pair, :, 0:128] += dot(grad_scores, self.queries_along[i])
        across = jnp.concatenate(
            [self.across[layer, pair * 2, 0:128], self.across[layer, pair * 2 + 1, 0:128]], axis=1
        )
        for head in range(2):
            rows = slice(head * 64, head * 64 + 64)
            self.grad_queries[i, rows] += dot(across[rows], grad_scores[:, head * 256 : head * 256 + 256])

    def half_of_pair(self, i, zh):
        return self.pair_grads[i, pl.ds(pl.multiple_of(zh * 256, 256), 256)]

    def send_pair(self, k):
        i = step(self.here.y, ORDER[k])
        self.sent_grads[i] = self.half_of_pair(i, 1 - self.here.zh).astype(BF16)
        self.swap.post(k, self.sent_grads.at[i])

    def relay_pair(self, layer, k):
        i = step(self.here.y, ORDER[k])
        self.swap.relay(k, lambda zh: self.other_grads.at[layer, i])

    def grad_project(self, layer, i):
        cosine, sine = self.angles[self.here.zh, 0, i], self.angles[self.here.zh, 1, i]
        summed = (self.half_of_pair(i, self.here.zh) + self.other_grads[layer, i].astype(F32)).T
        for head in range(2):
            rows = slice(head * 64, head * 64 + 64)
            self.into_in[i, head, 0:64] = turn(
                self.grad_queries[i, rows] * HD**-0.5, cosine, -sine
            ).astype(BF16)
            self.into_in[i, head, 64:128] = turn(summed[rows], cosine, -sine).astype(BF16)
            self.into_in[i, head, 128:192] = summed[128 + head * 64 : 192 + head * 64].astype(BF16)

    def keep_unit_sums(self, layer):
        ones = jnp.ones((8, 256), BF16)
        for zh in range(2):
            value = sum(dot(ones, self.into_in[i, zh], 1, 1) for i in range(4))[0:1]
            value = jnp.concatenate([value, jnp.zeros((1, 64), F32)], axis=1)
            for k in range(4):
                row = 48 + (layer * 2 + zh) * 4 + k
                self.vectors[0, row : row + 1, :] = value[:, k * 128 : k * 128 + 128]

    def weight_grads_out(self, layer):
        self.weight_grads(
            layer,
            lambda zh: jnp.concatenate([self.into_out[layer, i, zh] for i in range(4)], axis=1),
            self.grad_rows,
            OUT_ROWS,
        )

    def weight_grads_in(self, layer, rows):
        self.weight_grads(
            layer,
            lambda zh: jnp.concatenate([self.into_in[i, zh, rows] for i in range(4)], axis=1),
            self.rows,
            rows,
        )

    def backward(self, layer, hooks, fill):
        self.swap = Swap(self.here, self.mail, self.relays.at[LAYERS - 1 - layer])
        reduce = self.rows_reduce()
        if layer == LAYERS - 1:
            pl.semaphore_wait(self.credit, 3)

        def after(k):
            def run():
                self.send_pair(k)
                if k < 3:
                    hooks[k]()

            return run

        def attention(k, _):
            def unit(i, pair, later):
                self.attend_back(layer, i, pair)
                for m in range(1, 4):
                    due = min(m + 1, 3)
                    pl.when(jnp.logical_and(k == m, later == due))(lambda m=m: self.relay_pair(layer, m - 1))

            self.each_unit(k, unit)
            at_step(k, [after(m) for m in range(4)])
            return 0

        def first():
            self.swap.arrived(0)

        def second():
            self.swap.arrived(1)

        def third():
            self.relay_pair(layer, 3)
            self.swap.arrived(2)

        def fourth():
            fill[0]()
            self.swap.arrived(3)

        def second_out():
            reduce.chunk(ORDER[1])
            reduce.send_far()

        def third_out():
            reduce.chunk(ORDER[2])
            reduce.send_right()

        def fourth_out():
            reduce.chunk(ORDER[3])
            reduce.send_left()

        def rows_of(n, _):
            i = self.ordered(n)
            at_step(n, [first, second, third, fourth])
            self.grad_project(layer, i)
            self.spread_rows(i, self.into_in[i].reshape(896, 256), layer, IN_ROWS)
            at_step(n, [lambda: reduce.chunk(ORDER[0]), second_out, third_out, fourth_out])
            return 0

        def both(k, _):
            @pl.when(k == 3)
            def _():
                rows_of(0, 0)

            return attention(k, 0)

        lax.fori_loop(0, 4, both, 0)
        lax.fori_loop(1, 4, rows_of, 0)
        fill[1]()
        return reduce

    def norm_back(self, layer, half, grad_normed, sums):
        rows = slice(half * 64, half * 64 + 64)
        normal, inverse = self.normal[layer, rows], self.inverse[layer, rows, 0:1]
        sums[0] = sums[0] + jnp.sum(grad_normed * normal, axis=0, keepdims=True)
        sums[1] = sums[1] + jnp.sum(grad_normed, axis=0, keepdims=True)
        scaled = grad_normed * self.vector(self.gain, layer)
        first_mean = jnp.mean(scaled, axis=-1, keepdims=True)
        cross_mean = jnp.mean(scaled * normal, axis=-1, keepdims=True)
        return self.stream[rows] + inverse * (scaled - first_mean - normal * cross_mean)

    def round_rows(self, layer, half, grad, sums):
        rows = slice(half * 64, half * 64 + 64)
        low = grad.astype(BF16)
        self.grad_rows[layer, self.here.y, self.here.core, rows] = low
        sums[2] = sums[2] + jnp.sum(low.astype(F32), axis=0, keepdims=True)

    def weight_reduce(self, part, begin, first, second, name):
        slots = [getattr(self, name + "_" + kind) for kind in ("z", "x", "third", "fourth")]
        return WeightReduce(self.here, self.mail, part, begin, first, second, slots)

    def sum_vectors(self, begin, count, kept):
        here, mail = self.here, self.mail
        summed = count - kept
        rows = pl.ds(begin, count)

        def slot(k):
            return self.vector_slots.at[k, rows]

        for stage, axis in enumerate(("dx", "dz")):
            posts = [
                mail.post(self.vectors.at[stage, rows], slot(3 * stage + d - 1), here.at(**{axis: d}))
                for d in (1, 2, 3)
            ]
            yield
            mail.take(*posts)
            self.vectors[stage + 1, rows] = self.vectors[stage, rows] + sum(
                slot(3 * stage + d)[...] for d in range(3)
            )
        posts = [
            mail.post(self.vectors.at[2, rows], slot(6 + d - 1), here.at(dy=d)) for d in (1, 2, 3)
        ]
        yield
        mail.take(*posts)
        whole = self.vector_whole
        self.vector_whole[0, begin : begin + summed] = self.vectors[2, begin : begin + summed] + sum(
            self.vector_slots[6 + d, begin : begin + summed] for d in range(3)
        )
        total = summed
        if kept:
            total = summed + 4 * kept
            first, last = begin + summed, begin + count
            whole[0, pl.ds(first + here.y * kept, kept)] = self.vectors[2, first:last]
            for d in (1, 2, 3):
                whole[0, pl.ds(first + step(here.y, -d) * kept, kept)] = self.vector_slots[
                    6 + d - 1, first:last
                ]
        rows_out = pl.ds(begin, total)
        last = mail.post(whole.at[0, rows_out], whole.at[1, rows_out], self.partner)
        yield
        mail.take(last)
        yield

    def write_vectors(self, whole):
        for kind, out in enumerate((self.gain_out, self.shift_out, self.bias_out)):
            for layer in range(LAYERS):
                for s in range(8):
                    row = vector_row(kind, layer) + s
                    out[layer : layer + 1, s * 128 : s * 128 + 128] = (
                        whole[0, row : row + 1] + whole[1, row : row + 1]
                    )
        for source in range(2):
            core = self.here.core if source == 0 else 1 - self.here.core
            for y in range(4):
                for layer in range(LAYERS):
                    for zh in range(2):
                        head = y * 4 + zh * 2 + core
                        row = 48 + y * 16 + (layer * 2 + zh) * 4
                        wide = jnp.concatenate(
                            [whole[source, row + k : row + k + 1] for k in range(4)], axis=1
                        )
                        self.qkv_bias_out[layer, pl.ds(head, 1), :] = wide[:, 0:192]
                        self.fc1_bias_out[
                            layer : layer + 1, pl.ds(pl.multiple_of(head * 256, 256), 256)
                        ] = wide[:, 192:448]

    def write_weights(self, layer, rows):
        owned = self.owned.at[layer]
        if rows == IN_ROWS:
            self.qkv_out[layer] = owned[0:192]
            return
        self.fc1_out[layer] = owned[192:448].T
        self.out_out[layer] = owned[448:512]
        self.fc2_out[layer] = owned[512:768]


    def run(self):
        here, mail = self.here, self.mail
        barrier = pltpu.get_barrier_semaphore()
        everyone = self.near_x + self.near_y + self.near_z + [self.partner] + self.far
        tell(barrier, everyone)
        self.prepare(0)
        self.prepare_mask()
        self.stream[...] = self.arrange(self.hidden_in).astype(F32)
        for half in range(2):
            self.norm(0, half)
        zero = jnp.zeros((1, 1024), F32)
        sums = [zero, zero, zero]
        for half in range(2):
            self.round_rows(
                1, half, self.arrange(self.cotangent.at[half * 64 : half * 64 + 64]).astype(F32), sums
            )
        self.keep_sum(2, 1, sums[2])
        pl.semaphore_wait(barrier, len(everyone))

        def gather_weights(layer, begin, first, second):
            return WeightGather(here, mail, self.weights.at[layer], begin, first, second)

        def nothing():
            pass

        ahead = gather_weights(0, 0, 48, 48)
        rest = gather_weights(0, 192, 64, 224)
        later = gather_weights(1, 0, 192, 192)
        ahead.start()
        gather = RowsGather(here, mail, self.rows.at[0])
        gather.start()
        rest.start()
        self.prepare_bias(0)
        ahead.relay()
        ahead.turn()
        rest.relay()
        back = RowsGather(here, mail, self.grad_rows.at[1])
        ahead.late()
        gather.relay()
        rest.turn((1,))
        ahead.end()

        def after_near():
            self.swap_relay(0, 0)

        def after_far():
            self.swap_relay(0, 1)
            rest.late((1,))
            self.swap_relay(0, 2)

        self.project_all(0, gather, [nothing, nothing, after_near, after_far])
        back.start()
        self.clear_attention()
        self.prepare(1)
        self.swap_relay(0, 3)
        rest.turn((0,))
        self.swapped(0)

        def first_units():
            rest.late((0,))
            back.relay()

        def first_units_of(pair, _):
            self.units(0, pair)
            return 0

        def fourth_units():
            rest.end()
            later.start()
            lax.fori_loop(0, 2, first_units_of, 0)

        reduce = self.mix(
            0,
            {
                (0, 0): first_units,
                (0, 2): back.near,
                (0, 3): fourth_units,
                (1, 1): later.relay,
                (1, 2): back.far,
                (2, 2): later.turn,
                (3, 3): later.late,
            },
        )
        self.reduced = len(mail.forms)
        gather = RowsGather(here, mail, self.rows.at[1])
        for half, value in reduce.totals():
            rows = slice(half * 64, half * 64 + 64)
            bias = self.vector(self.out_bias, 0) + self.vector(self.fc2_bias, 0)
            self.stream[rows] = self.stream[rows] + value + bias
            self.norm(1, half)
            gather.start_half(half)
        later.end()
        for d in (0, -1, 1, 2):
            back.ready(d)
        self.prepare_bias(1)
        self.clear_attention()

        def ahead_of(n, _):
            self.grads_ahead(1, n)
            at_step(n, [gather.relay])
            return 0

        lax.fori_loop(0, 2, ahead_of, 0)
        self.project_all(
            1,
            gather,
            [
                nothing,
                lambda: self.swap_relay(1, 0),
                lambda: self.swap_relay(1, 1),
                lambda: self.swap_relay(1, 2),
            ],
        )

        def units_of(pair, _):
            self.units(1, pair)
            at_step(pair, [lambda: self.swap_relay(1, 3)])
            return 0

        lax.fori_loop(0, 2, units_of, 0)
        self.swapped(1)
        reduce = self.mix(1, {})
        self.clear_grads()

        def slope_of(i, _):
            self.slope_after(1, i)
            return 0

        lax.fori_loop(0, 4, slope_of, 0)
        for half, value in reduce.totals():
            rows = slice(half * 64, half * 64 + 64)
            bias = self.vector(self.out_bias, 1) + self.vector(self.fc2_bias, 1)
            self.restore(self.hidden_out.at[rows], (self.stream[rows] + value + bias).astype(BF16))
        self.reduced = len(mail.forms)
        tell(self.credit, self.near_y + [self.partner])

        self.stream[...] = self.arrange(self.cotangent).astype(F32)
        units = slice(192, 448)
        reduce = self.backward(
            1,
            [nothing] * 3,
            [lambda: self.weight_grads_out(1), lambda: self.weight_grads_in(1, units)],
        )
        self.reduced = len(mail.forms)
        sums = [zero, zero, zero]
        gather = RowsGather(here, mail, self.grad_rows.at[0])
        for half, value in reduce.totals():
            rows = slice(half * 64, half * 64 + 64)
            grad = self.norm_back(1, half, value, sums)
            self.round_rows(0, half, grad, sums)
            gather.start_half(half)
            self.stream[rows] = grad
        self.weight_grads_in(1, slice(0, 192))
        whole = self.weight_reduce(self.weight_part.at[1], 0, 192, 192, "whole")
        whole.start()
        self.keep_unit_sums(1)
        gather.relay()
        self.keep_sum(0, 1, sums[0])
        self.keep_sum(1, 1, sums[1])
        self.keep_sum(2, 0, sums[2])
        self.clear_grads()
        gather.near()

        def first_pair():
            for d in (0, -1, 1):
                gather.ready(d)

        def other_pair():
            gather.far()
            gather.ready(2)

        def grads_of(n, _):
            at_step(n, [first_pair, other_pair])
            self.grads_now(0, lax.rem(lax.div(here.y, 2) + n, 2))
            return 0

        whole.relay()
        lax.fori_loop(0, 2, grads_of, 0)
        self.weight_grads_out(0)
        self.weight_grads_in(0, units)
        whole.turn()
        early = self.weight_reduce(self.weight_part.at[0], 192, 64, 224, "early")
        early.start()
        late = self.weight_reduce(self.weight_part.at[0], 0, 48, 48, "late")

        def first_hook():
            whole.late()

        def second_hook():
            early.relay()

        def third_hook():
            whole.end(self.owned.at[1])
            self.write_weights(1, IN_ROWS)
            self.write_weights(1, OUT_ROWS)

        def first_fill():
            pass

        def second_fill():
            early.turn()
            self.weight_grads_in(0, slice(0, 192))
            late.start()
            self.keep_unit_sums(0)

        reduce = self.backward(0, [first_hook, second_hook, third_hook], [first_fill, second_fill])
        vectors = self.sum_vectors(16, 48, 16)
        next(vectors)
        early.late()
        sums = [zero, zero, zero]
        for half, value in reduce.totals():
            rows = slice(half * 64, half * 64 + 64)
            self.restore(self.grad_in.at[rows], self.norm_back(0, half, value, sums))
        self.keep_sum(0, 0, sums[0])
        self.keep_sum(1, 0, sums[1])
        last = self.sum_vectors(0, 16, 0)
        next(last)
        next(vectors)
        late.relay()
        early.end(self.owned.at[0])
        self.write_weights(0, OUT_ROWS)
        next(last)
        next(vectors)
        late.turn()
        next(last)
        next(vectors)
        late.late()
        next(last)
        next(vectors)
        late.end(self.owned.at[0])
        self.write_weights(0, IN_ROWS)
        next(last)
        self.write_vectors(self.vector_whole)
        mail.finish()


INPUTS = (
    "hidden_in", "cotangent", "qkv_weight", "fc1_weight", "out_weight", "fc2_weight",
    "gain", "shift", "qkv_bias", "fc1_bias", "out_bias", "fc2_bias", "angles",
)
OUTPUTS = {
    "hidden_out": ((128, 1024), BF16),
    "grad_in": ((128, 1024), F32),
    "gain_out": ((LAYERS, 1024), F32),
    "shift_out": ((LAYERS, 1024), F32),
    "qkv_out": ((LAYERS, 192, 128), F32),
    "qkv_bias_out": ((LAYERS, 16, 192), F32),
    "out_out": ((LAYERS, 64, 128), F32),
    "bias_out": ((LAYERS, 1024), F32),
    "fc1_out": ((LAYERS, 128, 256), F32),
    "fc1_bias_out": ((LAYERS, 4096), F32),
    "fc2_out": ((LAYERS, 256, 128), F32),
}
SCRATCH = {
    "weights": ((LAYERS, 4, 2, 2, 768, 128), BF16),
    "rows": ((LAYERS, 4, 2, 128, 1024), BF16),
    "grad_rows": ((LAYERS, 4, 2, 128, 1024), BF16),
    "stream": ((128, 1024), F32),
    "normal": ((LAYERS, 128, 1024), F32),
    "inverse": ((LAYERS, 128, 128), F32),
    "queries": ((LAYERS, 4, 128, 512), BF16),
    "across": ((LAYERS, 8, 256, 256), BF16),
    "along": ((LAYERS, 8, 256, 256), BF16),
    "slope": ((LAYERS, 4, 2, 256, 256), BF16),
    "into_out": ((LAYERS, 4, 2, 320, 256), BF16),
    "logs": ((LAYERS, 4, 8, 512), F32),
    "peaks": ((4, 8, 512), F32),
    "mask": ((2, 512, 256), F32),
    "totals": ((4, 8, 512), F32),
    "mixed": ((4, 128, 256), F32),
    "part": ((4, 2, 128, 1024), BF16),
    "from_partner": ((4, 128, 1024), BF16),
    "summed": ((4, 128, 1024), BF16),
    "slots": ((6, 64, 1024), BF16),
    "relays": ((2, 4, 256, 256), BF16),
    "delta": ((4, 8, 512), F32),
    "mixed_grads": ((4, 128, 512), BF16),
    "mixed_grads_along": ((4, 512, 128), BF16),
    "queries_along": ((4, 512, 128), BF16),
    "grad_queries": ((4, 128, 256), F32),
    "pair_grads": ((4, 512, 256), F32),
    "bias": ((2, 448, 8), F32),
    "owned": ((LAYERS, 768, 128), F32),
    "sent_grads": ((4, 256, 256), BF16),
    "other_grads": ((LAYERS, 4, 256, 256), BF16),
    "into_in": ((4, 2, 448, 256), BF16),
    "weight_part": ((LAYERS, 4, 2, 2, 768, 128), BF16),
    **reduce_slots("whole", 192, 192),
    **reduce_slots("early", 64, 224),
    **reduce_slots("late", 48, 48),
    "vectors": ((3, 64, 128), F32),
    "vector_slots": ((9, 64, 128), F32),
    "vector_whole": ((2, 112, 128), F32),
}
COPIES = 384


def kernel(*refs):
    names = (*INPUTS, *OUTPUTS, *SCRATCH, "send", "receive", "credit")
    Program(dict(zip(names, refs, strict=True))).run()


def hand_out(*refs):
    count = len(OUTPUTS)
    sources = [*refs[:count], refs[list(OUTPUTS).index("bias_out")]]
    for source, target in zip(sources, refs[count:], strict=True):
        target[...] = source[...]


def rotary_tables():
    frequency = 1.0 / 10000.0 ** (np.arange(0, ROT, 2).astype(np.float32) / np.float32(ROT))
    positions = (
        np.arange(4)[None, :, None] * 512 + np.arange(2)[:, None, None] * 256 + np.arange(256)
    ).astype(np.float32)
    angles = (positions[:, :, None, :] * frequency.astype(np.float32)[:, None]).astype(np.float64)
    return np.stack([np.cos(angles), np.sin(angles)], axis=1).astype(np.float32)


def on_device(
    hidden_in,
    ln_gain,
    ln_bias,
    qkv_weight,
    qkv_bias,
    out_weight,
    out_bias,
    fc1_weight,
    fc1_bias,
    fc2_weight,
    fc2_bias,
    cotangent,
):
    vmem = pl.BlockSpec(memory_space=pltpu.VMEM)
    shapes = [jax.ShapeDtypeStruct(*spec) for spec in OUTPUTS.values()]
    results = pl.pallas_call(
        kernel,
        out_shape=shapes,
        in_specs=[vmem] * len(INPUTS),
        out_specs=[vmem] * len(OUTPUTS),
        scratch_shapes=[pltpu.VMEM(*spec) for spec in SCRATCH.values()]
        + [pltpu.SemaphoreType.DMA((COPIES,))] * 2
        + [pltpu.SemaphoreType.REGULAR],
        compiler_params=pltpu.CompilerParams(
            collective_id=1, has_side_effects=True, vmem_limit_bytes=VMEM_LIMIT
        ),
    )(
        hidden_in[0],
        cotangent[0],
        qkv_weight.transpose(0, 2, 3, 1).reshape(LAYERS, 192, 128),
        fc1_weight,
        out_weight.reshape(LAYERS, 64, 128),
        fc2_weight,
        ln_gain,
        ln_bias,
        qkv_bias,
        fc1_bias,
        out_bias,
        fc2_bias,
        jnp.asarray(rotary_tables()),
    )
    bias = list(OUTPUTS).index("bias_out")
    sources = [*range(len(shapes)), bias]
    results = pl.pallas_call(
        hand_out,
        out_shape=[shapes[k] for k in sources],
        in_specs=[vmem] * len(shapes),
        out_specs=[vmem] * len(sources),
    )(*results)
    hidden_out, grad_in, gain, shift, qkv, qkv_sum, out, first, fc1, fc1_sum, fc2, second = results
    return (
        hidden_out[None],
        grad_in[None],
        gain,
        shift,
        qkv.reshape(LAYERS, 1, 192, 128).transpose(0, 3, 1, 2),
        qkv_sum,
        out.reshape(out_weight.shape),
        first,
        fc1,
        fc1_sum,
        fc2,
        second,
    )


def solution(mesh):
    placed = (
        P("shards", "context", None),
        P(),
        P(),
        P(None, "shards", "context", None),
        P(),
        P(None, "context", None, "shards"),
        P(),
        P(None, "shards", "context"),
        P(),
        P(None, "context", "shards"),
        P(),
        P("shards", "context", None),
    )
    return jax.shard_map(
        on_device,
        mesh=mesh,
        in_specs=placed,
        out_specs=(
            P("shards", "context", None),
            P("shards", "context", None),
            P(),
            P(),
            P(None, "shards", "context", None),
            P(),
            P(None, "context", None, "shards"),
            P(),
            P(None, "shards", "context"),
            P(),
            P(None, "context", "shards"),
            P(),
        ),
        check_vma=False,
    )
```

time: 1220 us -> 209 us (0.17)
  waiting for transfers between devices: 755 us -> 0 us
  Pallas kernels: 0 us -> 208 us
  blocking collectives: 188 us -> 0 us
  matrix products: 109 us -> 0 us
  other arithmetic: 78.8 us -> 0 us
  local copies, waits for them, and re-layouts: 60 us -> 0 us
  between operations: 16.6 us -> 0.78 us
    psum x4 -> x0, waiting for transfers between devices: 539 us -> none  [the longest x2 280 us: on_device(): lax.psum(branch_rows(mixed_low, active_low, full_weights[1], full_weights...]
    pallas_call x0 -> x2, Pallas kernels: none -> 208 us  [the longest x1 205 us: on_device(): pl.pallas_call(kernel, out_shape=shapes, in_specs=[vmem] * len(INPUTS), o...]
    all_gather x8 -> x0, blocking collectives: 188 us -> none  [the longest x2 51.9 us: on_device(): lax.all_gather(fc1_weight[layer_index], 'shards', axis=0, tiled=True)]
    unnamed x20 -> x0, waiting for transfers between devices: 140 us -> none
    dot_general x72 -> x0, matrix products: 109 us -> none  [the longest x2 13.8 us: forward_local(): jnp.dot(normed_low, w_up, preferred_element_type=jnp.float32) + bias_up]
    reduce_scatter x2 -> x0, waiting for transfers between devices: 76 us -> none  [on_device(): lax.psum_scatter(grad_w_up.astype(jnp.bfloat16), 'shards', scatter_dimens...]
    unnamed x316 -> x0, local copies, waits for them, and re-layouts: 42.1 us -> none
    reduce_sum x20 -> x0, other arithmetic: 31.8 us -> none  [the longest x2 11.5 us: norm_back(): first_mean = jnp.mean(scaled, axis=-1, keepdims=True)]
  transfers between devices with their start and end apart: 14 -> 0, of which waited for: 10 -> 0; matrix products, arithmetic and copies ran while one was open for 13% -> 0% of each run, Pallas kernels for 0% -> 0%
where the time goes in v1:
time: 209 us
  Pallas kernels  208 us (100%)
    pallas_call x1, Pallas kernels, on_device(): pl.pallas_call(kernel, out_shape=shapes, in_specs=[vmem] * len(INPUTS), o...  205 us

profile of v1, /device:TPU:1, one launch (start us, length us, event | category | flops | bytes accessed | tf_op | source)
XLA Modules:
  0.0 208.8 jit_solution(11375032109820900680)
XLA Ops:
  0.6 205.4 %shard_map.220 = (bf16[128,1024]{1,0:T(8,128)(2,1)}, f32[128,1024]{1,0:T(8,128)}, f32[2,1024]{1,0:T(2,128)}, f32[2,1024]{1,0:T(2,128)}, f32[2,192,128]{2,1,0:T(8...) custom-call(bf16[128,1024]{1,0:T(8,128)(2,1)} %bitcast.18, ...), custom_call_target="tpu_custom_call" | custom-call | tf_op jit(solution)/shard_map/pallas_call | solution.py:1326
  206.1 2.6 %shard_map.221 = (bf16[128,1024]{1,0:T(8,128)(2,1)}, f32[128,1024]{1,0:T(8,128)}, f32[2,1024]{1,0:T(2,128)}, f32[2,1024]{1,0:T(2,128)}, f32[2,192,128]{2,1,0:T(8...) custom-call(bf16[128,1024]{1,0:T(8,128)(2,1)} %get-tuple-element.35., ...), custom_call_target="tpu_custom_call" | custom-call | tf_op jit(solution)/shard_map/pallas_call | solution.py:1354
